TPU v7x, 32 devices: a whole 2x2x4 slice. The times are simulated.
32 devices in a mesh: row: 4 (over z), col: 8 (over y, x, core).
Axes of the slice: x: 2, y: 2, z: 4, core: 2. Of those that a mesh axis runs over, the one named last changes fastest.
Arguments:
- front: bfloat16 [32, 4, 128, 16, 8, 128], P(None, 'row', None, None, 'col'), may hold values from -8 to 25, as said below
- child_tiles: bfloat16 [1024, 128, 128], P(('row', 'col')), may hold values from -6 to 6
- tile_map: int32 [1024, 2], P(('row', 'col')), may hold values from 0 to 127, as said below
Outputs:
- factored: float32 [32, 4, 128, 16, 8, 128], P(None, 'row', None, None, 'col')
Inputs may be any that keep to these rules, and one draw needn't show every extreme that they name: The leading 2048 x 2048 block of front is symmetric positive definite. `tile_map`: each row names a parent row tile outside the first 16 row tiles; column tiles may be any, the panel's included. The owner of tile (i, j) is the device at row i % 4 and column j % 8; the 32 tiles of one device send at most 2 tiles to any one owner, and in every draw some owner receives 2 tiles from every device.
All inputs are finite; a program needn't handle non-finite values.
Results may differ from a plain program's by a relative error of at most 0.0013.
Values may be sent and summed in bfloat16 or wider, within the bound.
A program may use at most 384 MiB of HBM per device.

v0:
```python
import jax
import jax.numpy as jnp
from jax import lax
from jax.sharding import PartitionSpec as P

PANEL = 2048
CAP = 2


def spread(block, axis, source):
    block = jnp.where(lax.axis_index(axis) == source, block, jnp.zeros_like(block))
    return lax.psum(block, axis)


def per_device(front, child_tiles, tile_map):
    rows_local = front.shape[0]
    tile_size = front.shape[2]
    cols_local = front.shape[3]
    row_count = lax.axis_size("row")
    col_count = lax.axis_size("col")
    device_count = row_count * col_count
    row_index = lax.axis_index("row")
    col_index = lax.axis_index("col")
    panel_tiles = PANEL // tile_size
    corner_rows = panel_tiles // row_count
    corner_cols = panel_tiles // col_count
    owners = tile_map[:, 0] % row_count * col_count + tile_map[:, 1] % col_count
    local_ids = tile_map[:, 0] // row_count * cols_local + tile_map[:, 1] // col_count
    owner_hits = (owners[:, None] == jnp.arange(device_count)[None, :]).astype(jnp.int32)
    slot_rank = jnp.sum(jnp.cumsum(owner_hits, 0) * owner_hits, 1) - 1
    slot_index = owners * CAP + slot_rank
    packed = (
        jnp.zeros((device_count * CAP, tile_size, tile_size), jnp.bfloat16)
        .at[slot_index]
        .set(child_tiles)
    )
    targets = jnp.full((device_count * CAP,), -1, jnp.int32).at[slot_index].set(local_ids)
    arrived, arrived_ids = (
        lax.all_to_all(
            packed.reshape(device_count, CAP, tile_size, tile_size),
            ("row", "col"),
            split_axis=0,
            concat_axis=0,
            tiled=True,
        ),
        lax.all_to_all(
            targets.reshape(device_count, CAP),
            ("row", "col"),
            split_axis=0,
            concat_axis=0,
            tiled=True,
        ),
    )
    flat_tiles = arrived.reshape(device_count * CAP, tile_size * tile_size)
    flat_ids = arrived_ids.reshape(device_count * CAP)
    selector = (flat_ids[None, :] == jnp.arange(rows_local * cols_local)[:, None]).astype(
        jnp.bfloat16
    )
    added = jnp.dot(selector, flat_tiles, preferred_element_type=jnp.float32)
    added = added.reshape(rows_local, cols_local, tile_size, tile_size).transpose(0, 2, 1, 3)
    assembled = (
        front.reshape(rows_local, tile_size, cols_local, tile_size).astype(jnp.float32) + added
    ).astype(jnp.bfloat16)
    corner = assembled[:corner_rows, :, :corner_cols, :].reshape(
        corner_rows, 1, tile_size, corner_cols, 1, tile_size
    )
    corner = lax.all_gather(corner, "row", axis=1, tiled=True)
    corner = lax.all_gather(corner, "col", axis=4, tiled=True)
    lower_factor = jnp.linalg.cholesky(corner.reshape(PANEL, PANEL).astype(jnp.float32))
    panel_part = assembled[:, :, :corner_cols, :].reshape(
        rows_local, tile_size, corner_cols, 1, tile_size
    )
    share_tiles = rows_local // col_count
    mine = lax.all_to_all(panel_part, "col", split_axis=0, concat_axis=3, tiled=True)
    solved = lax.linalg.triangular_solve(
        lower_factor,
        mine.reshape(share_tiles * tile_size, PANEL).astype(jnp.float32),
        left_side=False,
        lower=True,
        transpose_a=True,
    )
    first_tile = col_index * share_tiles
    global_rows = ((first_tile + jnp.arange(share_tiles)) * row_count + row_index)[
        :, None
    ] * tile_size + jnp.arange(tile_size)[None, :]
    global_rows = global_rows.reshape(-1)
    known = lower_factor[jnp.minimum(global_rows, PANEL - 1)]
    solved_part = jnp.where((global_rows < PANEL)[:, None], known, solved).astype(jnp.bfloat16)
    row_panel = lax.all_gather(
        solved_part.reshape(share_tiles, tile_size, PANEL), "col", axis=0, tiled=True
    )
    row_panel = row_panel.reshape(rows_local * tile_size, PANEL)
    group_size = col_count // row_count
    picked = row_panel.reshape(cols_local, group_size, tile_size, PANEL)
    picked = lax.dynamic_index_in_dim(picked, col_index // row_count, 1, keepdims=False)
    col_panel = spread(picked, "row", col_index % row_count).reshape(cols_local * tile_size, PANEL)
    lower_rows = row_panel[corner_rows * tile_size :]
    right_cols = col_panel[corner_cols * tile_size :]
    update = lax.dot_general(
        lower_rows, right_cols, (((1,), (1,)), ((), ())), preferred_element_type=jnp.float32
    )
    trailing = assembled[corner_rows:, :, corner_cols:, :].astype(jnp.float32)
    trailing = trailing - update.reshape(
        rows_local - corner_rows, tile_size, cols_local - corner_cols, tile_size
    )
    panel_values = lax.dynamic_index_in_dim(
        row_panel.reshape(rows_local, tile_size, corner_cols, col_count, tile_size),
        col_index,
        3,
        keepdims=False,
    ).astype(jnp.float32)
    upper_zero = jnp.zeros(
        (corner_rows, tile_size, cols_local - corner_cols, tile_size), jnp.float32
    )
    right_part = jnp.concatenate([upper_zero, trailing], 0)
    result = jnp.concatenate([panel_values, right_part], 2)
    return result.reshape(rows_local, 1, tile_size, cols_local, 1, tile_size)


def solution(mesh):
    in_specs = (
        P(None, "row", None, None, "col", None),
        P(("row", "col"), None, None),
        P(("row", "col"), None),
    )
    out_specs = P(None, "row", None, None, "col", None)
    return jax.shard_map(
        per_device, mesh=mesh, in_specs=in_specs, out_specs=out_specs, check_vma=False
    )
```

profile of v0, /device:TPU:2, one launch (start us, length us, event | category | flops | bytes accessed | tf_op | source)
XLA Modules:
  0.0 1557.5 jit_solution(12818817282319583952)
XLA Ops:
  31.1 47.0 %all-to-all-done.1 = bf16[32,2,128,128]{3,2,1,0:T(8,128)(2,1)S(1)} async-done(((bf16[32,2,128,128]{3,2,1,0:T(8,128)(2,1)}), bf16[32,2,128,128]{3,2,1,0:T(8,128)(2,1)S(1)}, u32[]{:S(2)}, u32[]{:S(2)}) %all-to-all-start.1) | async-done | bytes 2097184 | tf_op jit(solution)/shard_map/all_to_all | solution.py:39
  78.1 13.4 fusion
  93.6 27.5 %all-gather.9.cloned.1.call-done = bf16[4,512,2,128]{3,2,1,0:T(2,128)(2,1)} async-done(((bf16[4,128,2,128]{3,2,1,0:T(2,128)(2,1)}), bf16[4,512,2,128]{3,2,1,0:T(2,128)(2,1)}) %all-gather.9.cloned.1.call-update) | async-done | bytes 1048592 | tf_op jit(solution)/shard_map/all_gather | solution.py:67
  136.2 33.3 %all-to-all-done.2 = bf16[32,128,2,1,128]{4,2,1,3,0:T(2,128)(2,1)S(1)} async-done(((bf16[32,128,2,1,128]{4,2,1,3,0:T(2,128)(2,1)}), bf16[32,128,2,1,128]{4,2,1,3,0:T(2,128)(2,1)S(1)}, u32[]{:S(2)}, u32[]{:S(2)}) %all-to-all-start.2) | async-done | bytes 2097184 | tf_op jit(solution)/shard_map/all_to_all | solution.py:74
  178.7 21.7 %all-gather.5.cloned.1.call-done = bf16[4,4,128,2,8,128]{2,1,0,5,4,3:T(4,128)(2,1)} async-done(((bf16[4,4,128,2,1,128]{2,1,0,5,4,3:T(4,128)(2,1)}), bf16[4,4,128,2,8,128]{2,1,0,5,4,3:T(4,128)(2,1)}) %all-gather.5.cloned.1.call-update) | async-done | bytes 8388624 | tf_op jit(solution)/shard_map/all_gather | solution.py:68
  200.4 14.9 reshape.303
  215.3 17.6 %copy.88 = f32[2048,2048]{1,0:T(8,128)} copy(f32[2048,2048]{0,1:T(8,128)} %reshape.303) | data formatting | bytes 33554432 | tf_op jit(solution)/shard_map/convert_element_type | solution.py:69
  232.9 11.9 fusion.1
  250.5 11.7 cholesky.457
  285.6 11.9 cholesky.480
  313.2 11.7 cholesky.503
  342.5 11.7 cholesky.524
  372.0 11.7 cholesky.962
  401.7 11.9 cholesky.982
  431.9 11.7 cholesky.1002
  462.6 11.7 cholesky.1022
  492.8 11.7 cholesky.1042
  523.1 11.7 cholesky.1062
  553.1 11.7 cholesky.1082
  582.4 11.9 cholesky.1102
  611.3 11.7 cholesky.1122
  639.8 11.7 cholesky.1142
  667.0 11.9 cholesky.1162
  717.2 16.1 %fusion.2 = (f32[2048,2048]{1,0:T(8,128)}, bf16[2048,2048]{1,0:T(8,128)(2,1)}) fusion(f32[2048,2048]{1,0:T(8,128)} %get-tuple-element.135, pred[]{:T(512)S(6)} %cholesky.1203), kind=kLoop, calls=%fused_computation.14 | loop fusion | flops 20971520 | bytes 41943040 | tf_op jit(solution)/shard_map/triangular_solve | solution.py:75
  746.9 54.2 %while.1 = (s32[]{:T(128)}, f32[2048,2048]{1,0:T(8,128)}, s32[16,2]{0,1:T(2,128)S(1)}, f32[16,128,128]{2,1,0:T(8,128)}, s32[]{:T(128)}) while((s32[]{:T(128)}, f32[2048,2048]{1,0:T(8,128)}, s32[16,2]{0,1:T(2,128)S(1)}, f32[16,128,128]{2,1,0:T(8,128)}, s32[]{:T(128)}) %tuple.174), condition=%wide.while_cond, body=%wide.while_body.sunk | while | flops 2 | bytes 132205 | solution.py:75
  801.1 158.4 %custom-call.141 = f32[16,128,128]{1,2,0:T(8,128)S(1)} custom-call(f32[16,128,128]{2,1,0:T(8,128)} %get-tuple-element.12), custom_call_target="InvertDiagBlocksLowerTriangular" | custom-call | tf_op jit(solution)/shard_map/triangular_solve | solution.py:75
  1073.3 89.9 %all-gather.7.cloned.1.call-done = bf16[32,128,2048]{2,1,0:T(8,128)(2,1)} async-done(((bf16[4,128,2048]{2,1,0:T(8,128)(2,1)}), bf16[32,128,2048]{2,1,0:T(8,128)(2,1)}) %all-gather.7.cloned.1.call-update) | async-done | bytes 16777232 | tf_op jit(solution)/shard_map/all_gather | solution.py:89
  1170.4 22.5 %copy.109 = bf16[32,128,2048]{1,2,0:T(8,128)(2,1)} copy(bf16[32,128,2048]{2,1,0:T(8,128)(2,1)} %all-gather.7.cloned.1.call-done) | data formatting | bytes 33554432 | tf_op jit(solution)/shard_map/all_gather | solution.py:89
  1204.6 256.8 %all-reduce.4.cloned.1.call-done = bf16[16,128,2048]{2,1,0:T(8,128)(2,1)} async-done(((bf16[16,128,2048]{2,1,0:T(8,128)(2,1)}), bf16[16,128,2048]{2,1,0:T(8,128)(2,1)}) %all-reduce.4.cloned.1.call-update) | async-done | bytes 8388624 | tf_op jit(solution)/shard_map/psum | solution.py:12
  1461.5 34.3 %fusion.3 = f32[28,128,14,128]{3,1,2,0:T(8,128)} fusion(bf16[32,128,2048]{2,1,0:T(8,128)(2,1)} %all-gather.7.cloned.1.call-done, bf16[16,128,2048]{2,1,0:T(8,128)(2,1)} %all-reduce.4.cloned.1.call-done), kind=kOutput, calls=%fused_computation.16 | convolution fusion | flops 26306674688 | bytes 47710208 | tf_op jit(solution)/shard_map/dot_general | solution.py:99
  1495.8 30.8 %copy_subtract_fusion = f32[28,128,14,128]{3,2,1,0:T(8,128)} fusion(f32[28,128,14,128]{3,1,2,0:T(8,128)} %fusion.3, bf16[32,128,16,128]{3,2,1,0:T(8,128)(2,1)} %fusion), kind=kLoop, calls=%fused_computation.9 | loop fusion | flops 12845056 | bytes 64225280 | tf_op jit(solution)/shard_map/sub | solution.py:103
  1526.6 24.2 %select_maximum_fusion = f32[32,128,16,128]{3,2,1,0:T(8,128)} fusion(f32[28,128,14,128]{3,2,1,0:T(8,128)} %copy_subtract_fusion, f32[32,128,2,128]{3,2,1,0:T(2,128)S(1)} %copy-done.1), kind=kLoop, calls=%fused_computation.5 | loop fusion | flops 25165824 | bytes 63438848 | tf_op jit(solution)/shard_map/concatenate | solution.py:116
  (278 shorter events, 536.7 us)
Async XLA Ops:
  10.5 13.2 all-to-all-start
  23.7 54.4 %all-to-all-start.1 = ((bf16[32,2,128,128]{3,2,1,0:T(8,128)(2,1)}), bf16[32,2,128,128]{3,2,1,0:T(8,128)(2,1)S(1)}, u32[]{:S(2)}, u32[]{:S(2)}) async-start(bf16[32,2,128,128]{3,2,1,0:T(8,128)(2,1)} %bitcast.10), calls=%async_computation.1 | async-start | bytes 4194304 | tf_op jit(solution)/shard_map/all_to_all | solution.py:39
  29.6 91.6 %all-gather.9.cloned.1.call-start = ((), (), s32[]{:S(2)}) async-start(), calls=%async_computation.6 | async-start | bytes 1310720 | tf_op jit(solution)/shard_map/all_gather | solution.py:67
  93.6 106.9 %all-gather.5.cloned.1.call-start = ((), (), s32[]{:S(2)}) async-start(), calls=%async_computation.3 | async-start | bytes 9437184 | tf_op jit(solution)/shard_map/all_gather | solution.py:68
  131.8 37.7 %all-to-all-start.2 = ((bf16[32,128,2,1,128]{4,2,1,3,0:T(2,128)(2,1)}), bf16[32,128,2,1,128]{4,2,1,3,0:T(2,128)(2,1)S(1)}, u32[]{:S(2)}, u32[]{:S(2)}) async-start(bf16[32,128,2,1,128]{4,2,1,3,0:T(2,128)(2,1)} %slice_bitcast_fusion.4), calls=%async_computation.2 | async-start | bytes 4194304 | tf_op jit(solution)/shard_map/all_to_all | solution.py:74
  136.0 1027.2 %all-gather.7.cloned.1.call-start = ((), (), s32[]{:S(2)}) async-start(), calls=%async_computation.4 | async-start | bytes 18874368 | tf_op jit(solution)/shard_map/all_gather | solution.py:89
  244.8 5.7 copy-start
  959.4 42.3 %copy-start.4 = (f32[16,128,128]{1,2,0:T(8,128)}, f32[16,128,128]{1,2,0:T(8,128)S(1)}, u32[]{:S(2)}) copy-start(f32[16,128,128]{1,2,0:T(8,128)S(1)} %custom-call.141) | copy-start | bytes 3145732
  1003.6 5.8 copy-start.3
  1051.5 9.7 copy-start.5
  1051.5 9.7 copy-start.6
  1051.5 9.8 copy-start.7
  1051.5 9.8 copy-start.8
  1053.6 7.8 copy-start.9
  1053.6 7.8 copy-start.10
  1053.6 7.9 copy-start.11
  1053.6 7.9 copy-start.12
  1059.4 8.3 copy-start.2
  1061.2 5.1 copy-start.13
  1073.2 388.3 %all-reduce.4.cloned.1.call-start = ((), (), s32[]{:S(2)}) async-start(), calls=%async_computation.5 | async-start | bytes 16777216 | tf_op jit(solution)/shard_map/psum | solution.py:12
  1495.8 30.8 %copy-start.1 = (f32[32,128,2,128]{3,2,1,0:T(2,128)S(1)}, f32[32,128,2,128]{3,2,1,0:T(2,128)}, u32[]{:S(2)}) copy-start(f32[32,128,2,128]{3,2,1,0:T(2,128)} %bitcast_convert_fusion) | copy-start | bytes 12582916
Sparse Core Ops, SparseCore 0:
  93.7 27.4 all-gather.8
  125.2 75.1 all-gather.4
  1073.3 89.8 all-gather.6
  1170.6 290.8 all-reduce.3
where the time goes:
time: 1570 us; the launch traced here: 1560 us
  other arithmetic  616 us (39%)
  waiting for transfers between devices  476 us (30%)
  matrix products  226 us (14%)
  local copies, waits for them, and re-layouts  199 us (13%)
  between operations  24.1 us (2%)
  starting transfers between devices  16.3 us (1%)
    another operation x62, other arithmetic, per_device(): jnp.linalg.cholesky(corner.reshape(PANEL, PANEL).astype(jnp.float32))  356 us
    psum x1, waiting for transfers between devices, spread(): return lax.psum(block, axis)  257 us
    another operation x3, other arithmetic, per_device(): lax.linalg.triangular_solve(lower_factor, mine.reshape(share_tiles * tile...  174 us
    another operation x30, matrix products, per_device(): jnp.linalg.cholesky(corner.reshape(PANEL, PANEL).astype(jnp.float32))  92.2 us
    all_gather x1, waiting for transfers between devices, per_device(): lax.all_gather(solved_part.reshape(share_tiles, tile_size, PANEL), 'col',...  89.9 us
    another operation x31, matrix products, per_device(): lax.linalg.triangular_solve(lower_factor, mine.reshape(share_tiles * tile...  86.4 us
    another operation x48, local copies, waits for them, and re-layouts  54.2 us
    all_to_all x1, waiting for transfers between devices, per_device(): lax.all_to_all(packed.reshape(device_count, CAP, tile_size, tile_size), (...  47 us
  transfers between devices with their start and end apart: 7, of which 6 were waited for; matrix products, arithmetic and copies ran while one was open for 4% of the time, Pallas kernels for 0%

commit v1 on v0

v1 whole, which is shorter than its diff:
```python
import functools

import jax
import jax.numpy as jnp
from jax import lax
from jax.experimental import pallas as pl
from jax.experimental.pallas import tpu as pltpu
from jax.sharding import PartitionSpec as P

PANEL = 2048
CAP = 2
TILE = 128
STEP = 256
SUB = 8
VMEM_LIMIT = 56 * 1024 * 1024
NN = (((1,), (0,)), ((), ()))
NT = (((1,), (1,)), ((), ()))


def split(x):
    high = x.astype(jnp.bfloat16)
    low = (x - high.astype(jnp.float32)).astype(jnp.bfloat16)
    return high, low


def dot3(x, y, dims):
    xh, xl = split(x)
    yh, yl = split(y)
    dot = functools.partial(lax.dot_general, dimension_numbers=dims, preferred_element_type=jnp.float32)
    return dot(xh, yh) + (dot(xh, yl) + dot(xl, yh))


def factor_tile(s):
    n = s.shape[0]
    groups = n // SUB
    rows = lax.broadcasted_iota(jnp.int32, (SUB, n), 0)
    lanes = lax.broadcasted_iota(jnp.int32, (SUB, n), 1)
    left = [s[g * SUB : (g + 1) * SUB, :] for g in range(groups)]
    right = [(lanes == rows + g * SUB).astype(jnp.float32) for g in range(groups)]
    for g in range(groups):
        base = g * SUB
        r, e = left[g], right[g]
        cols = [jnp.broadcast_to(r[:, base + m : base + m + 1], (SUB, n)) for m in range(SUB)]
        u = jnp.zeros_like(r)
        v = jnp.zeros_like(e)
        u_rows, v_rows = [], []
        for i in range(SUB):
            inv = lax.rsqrt(jnp.broadcast_to(cols[i][i : i + 1, :], (SUB, n)))
            scaled = cols[i] * inv
            ru = jnp.broadcast_to(r[i : i + 1, :], (SUB, n)) * inv
            rv = jnp.broadcast_to(e[i : i + 1, :], (SUB, n)) * inv
            u_rows.append(ru)
            v_rows.append(rv)
            u = jnp.where(rows == i, ru, u)
            v = jnp.where(rows == i, rv, v)
            if i + 1 < SUB:
                r = r - scaled * ru
                e = e - scaled * rv
                for m in range(i + 1, SUB):
                    cols[m] = cols[m] - scaled * jnp.broadcast_to(scaled[m : m + 1, :], (SUB, n))
        left[g], right[g] = u, v
        if g + 1 < groups:
            ut = u.T
            for h in range(g + 1, groups):
                part = ut[h * SUB : (h + 1) * SUB, :]
                sh, eh = left[h], right[h]
                for m in range(SUB):
                    c = jnp.broadcast_to(part[:, m : m + 1], (SUB, n))
                    sh = sh - c * u_rows[m]
                    eh = eh - c * v_rows[m]
                left[h], right[h] = sh, eh
    upper = jnp.concatenate(left, 0)
    inverse = jnp.concatenate(right, 0)
    ri = lax.broadcasted_iota(jnp.int32, (n, n), 0)
    ci = lax.broadcasted_iota(jnp.int32, (n, n), 1)
    return jnp.where(ri <= ci, upper, 0.0), jnp.where(ri >= ci, inverse, 0.0)


def factor_kernel(row_count, col_count, blocks_ref, lower_ref, high_ref, low_ref, work_ref, inv_ref, q_ref):
    corner_rows = PANEL // TILE // row_count
    corner_cols = PANEL // TILE // col_count
    steps = PANEL // STEP
    half = STEP // 2

    def place(index, _):
        ri, ci = index // col_count, index % col_count
        for a in range(corner_rows):
            for b in range(corner_cols):
                r0 = pl.multiple_of((a * row_count + ri) * TILE, TILE)
                c0 = pl.multiple_of((b * col_count + ci) * TILE, TILE)
                work_ref[pl.ds(r0, TILE), pl.ds(c0, TILE)] = blocks_ref[
                    index, a * TILE : (a + 1) * TILE, b * TILE : (b + 1) * TILE
                ].astype(jnp.float32)
        return 0

    lax.fori_loop(0, row_count * col_count, place, 0)
    lower_ref[...] = jnp.zeros_like(lower_ref)

    def step(k, _):
        at = pl.multiple_of(k * STEP, STEP)
        here = pl.ds(at, STEP)
        s11 = work_ref[pl.ds(at, half), pl.ds(at, half)]
        up11, inv11 = factor_tile(s11)
        s21 = work_ref[pl.ds(at + half, half), pl.ds(at, half)]
        l21 = dot3(s21, inv11, NT)
        s22 = work_ref[pl.ds(at + half, half), pl.ds(at + half, half)] - dot3(l21, l21, NT)
        up22, inv22 = factor_tile(s22)
        inv21 = -dot3(inv22, dot3(l21, inv11, NN), NN)
        inv_ref[:half, :half] = inv11
        inv_ref[:half, half:] = jnp.zeros((half, half), jnp.float32)
        inv_ref[half:, :half] = inv21
        inv_ref[half:, half:] = inv22
        lower_ref[pl.ds(at, half), pl.ds(at, half)] = up11.T.astype(jnp.bfloat16)
        lower_ref[pl.ds(at + half, half), pl.ds(at, half)] = l21.astype(jnp.bfloat16)
        lower_ref[pl.ds(at + half, half), pl.ds(at + half, half)] = up22.T.astype(jnp.bfloat16)

        def block_row(j, _):
            cols = pl.ds(pl.multiple_of(j * STEP, STEP), STEP)
            q = dot3(inv_ref[...], work_ref[here, cols], NN)
            q = jnp.where(j == k, inv_ref[...], q)
            work_ref[here, cols] = q
            high, low = split(q)
            q_ref[0:STEP, cols] = high
            q_ref[STEP : 2 * STEP, cols] = low
            q_ref[2 * STEP :, cols] = high
            return 0

        lax.fori_loop(0, steps, block_row, 0)

        def below(i, _):
            mine = pl.ds(pl.multiple_of(i * STEP, STEP), STEP)
            p = dot3(work_ref[mine, here], inv_ref[...], NT)
            high, low = split(p)
            lower_ref[mine, here] = high
            work_ref[mine, here] = jnp.zeros((STEP, STEP), jnp.float32)
            wide = jnp.concatenate([high, high, low], 1)
            width = 2 * STEP
            for j in range(PANEL // width):
                cols = slice(j * width, (j + 1) * width)
                work_ref[mine, cols] = work_ref[mine, cols] - jnp.dot(
                    wide, q_ref[:, cols], preferred_element_type=jnp.float32
                )
            return 0

        lax.fori_loop(k + 1, steps, below, 0)
        return 0

    lax.fori_loop(0, steps, step, 0)

    def finish(i, _):
        mine = pl.ds(pl.multiple_of(i * TILE, TILE), TILE)
        rows = lax.broadcasted_iota(jnp.int32, (TILE, STEP), 0) + i * TILE
        lanes = lax.broadcasted_iota(jnp.int32, (TILE, STEP), 1)
        for j in range(steps):
            cols = slice(j * STEP, (j + 1) * STEP)
            high, low = split(jnp.where(rows >= lanes + j * STEP, work_ref[mine, cols], 0.0))
            high_ref[mine, cols] = high
            low_ref[mine, cols] = low
        return 0

    lax.fori_loop(0, PANEL // TILE, finish, 0)


def factor_corner(blocks, row_count, col_count):
    return pl.pallas_call(
        functools.partial(factor_kernel, row_count, col_count),
        out_shape=(jax.ShapeDtypeStruct((PANEL, PANEL), jnp.bfloat16),) * 3,
        in_specs=[pl.BlockSpec(memory_space=pltpu.VMEM)],
        out_specs=(pl.BlockSpec(memory_space=pltpu.VMEM),) * 3,
        scratch_shapes=[
            pltpu.VMEM((PANEL, PANEL), jnp.float32),
            pltpu.VMEM((STEP, STEP), jnp.float32),
            pltpu.VMEM((3 * STEP, PANEL), jnp.bfloat16),
        ],
        compiler_params=pltpu.CompilerParams(vmem_limit_bytes=VMEM_LIMIT),
        cost_estimate=pl.CostEstimate(flops=200 * 10**9, bytes_accessed=32 << 20, transcendentals=0),
        name="factor_corner",
    )(blocks)


def solve_kernel(col_count, parts_ref, high_ref, low_ref, out_ref, x_ref):
    tiles = parts_ref.shape[2] // TILE
    for b in range(tiles):
        for c in range(col_count):
            j = b * col_count + c
            x_ref[:, j * TILE : (j + 1) * TILE] = parts_ref[c, :, b * TILE : (b + 1) * TILE]
    for n in range(PANEL // STEP):
        end = (n + 1) * STEP
        rows = slice(n * STEP, end)
        x = x_ref[:, :end]
        y = lax.dot_general(x, high_ref[rows, :end], NT, preferred_element_type=jnp.float32)
        y = y + lax.dot_general(x, low_ref[rows, :end], NT, preferred_element_type=jnp.float32)
        out_ref[:, rows] = y.astype(jnp.bfloat16)


def solve_rows(parts, high, low, skip):
    col_count, rows, width = parts.shape
    chunk = 256 if rows % 256 == 0 and skip % 256 == 0 else TILE
    first = skip // chunk
    whole = pl.BlockSpec((PANEL, PANEL), lambda s: (0, 0))
    return pl.pallas_call(
        functools.partial(solve_kernel, col_count),
        grid=((rows - skip) // chunk,),
        out_shape=jax.ShapeDtypeStruct((rows - skip, PANEL), jnp.bfloat16),
        in_specs=[pl.BlockSpec((col_count, chunk, width), lambda s: (0, s + first, 0)), whole, whole],
        out_specs=pl.BlockSpec((chunk, PANEL), lambda s: (s, 0)),
        scratch_shapes=[pltpu.VMEM((chunk, PANEL), jnp.bfloat16)],
        compiler_params=pltpu.CompilerParams(vmem_limit_bytes=VMEM_LIMIT),
        cost_estimate=pl.CostEstimate(
            flops=2 * (rows - skip) * PANEL * PANEL, bytes_accessed=(rows - skip) * PANEL * 4, transcendentals=0
        ),
        name="solve_rows",
    )(parts, high, low)


def trailing_kernel(
    corner_rows, corner_cols, group, starts, order, spots, xr_ref, xc_ref, front_ref, own_ref, child_ref, out_ref
):
    step = pl.program_id(0)
    first = corner_rows // group

    @pl.when(step < first)
    def _():
        out_ref[...] = jnp.zeros_like(out_ref)

    @pl.when(step >= first)
    def _():
        out_ref[...] = front_ref[...].astype(jnp.float32)
        for part in range(group):
            rows = pl.ds(part * TILE, TILE)
            a = step * group + part

            def add(p, _):
                out_ref[rows, spots[p], :] = out_ref[rows, spots[p], :] + child_ref[order[p]].astype(jnp.float32)
                return 0

            lax.fori_loop(starts[a], starts[a + 1], add, 0)
        columns = out_ref.shape[1]
        for start in range(corner_cols, columns, 2):
            width = min(2, columns - start)
            at = (start - corner_cols) * TILE
            update = lax.dot_general(
                xr_ref[...],
                xc_ref[at : at + width * TILE, :],
                NT,
                preferred_element_type=jnp.float32,
            )
            for w in range(width):
                b = start + w
                out_ref[:, b, :] = (
                    out_ref[:, b, :].astype(jnp.bfloat16).astype(jnp.float32)
                    - update[:, w * TILE : (w + 1) * TILE]
                )

    for b in range(corner_cols):
        out_ref[:, b, :] = own_ref[:, b * TILE : (b + 1) * TILE].astype(jnp.float32)


def trailing_update(row_panel, col_panel, front, own, child, starts, order, spots, corner_rows, corner_cols):
    rows, cols_local, _ = front.shape
    group = 2 if corner_rows % 2 == 0 and rows // TILE % 2 == 0 else 1
    chunk = group * TILE
    first = corner_rows // group
    whole = lambda x: pl.BlockSpec(x.shape, lambda s, *_: (0,) * x.ndim)
    return pl.pallas_call(
        functools.partial(trailing_kernel, corner_rows, corner_cols, group),
        out_shape=jax.ShapeDtypeStruct((rows, cols_local, TILE), jnp.float32),
        grid_spec=pltpu.PrefetchScalarGridSpec(
            num_scalar_prefetch=3,
            grid=(rows // chunk,),
            in_specs=[
                pl.BlockSpec((chunk, PANEL), lambda s, *_: (jnp.maximum(s - first, 0), 0)),
                whole(col_panel),
                pl.BlockSpec((chunk, cols_local, TILE), lambda s, *_: (s, 0, 0)),
                pl.BlockSpec((chunk, corner_cols * TILE), lambda s, *_: (s, 0)),
                whole(child),
            ],
            out_specs=pl.BlockSpec((chunk, cols_local, TILE), lambda s, *_: (s, 0, 0)),
        ),
        compiler_params=pltpu.CompilerParams(vmem_limit_bytes=VMEM_LIMIT),
        name="trailing_update",
    )(starts, order, spots, row_panel, col_panel, front, own, child)


def per_device(front, child_tiles, tile_map):
    rows_local = front.shape[0]
    cols_local = front.shape[3]
    row_count = lax.axis_size("row")
    col_count = lax.axis_size("col")
    device_count = row_count * col_count
    row_index = lax.axis_index("row")
    col_index = lax.axis_index("col")
    panel_tiles = PANEL // TILE
    corner_rows = panel_tiles // row_count
    corner_cols = panel_tiles // col_count
    width = corner_cols * TILE
    front4 = front.reshape(rows_local, TILE, cols_local, TILE)

    corner = front4[:corner_rows, :, :corner_cols, :].reshape(corner_rows * TILE, width)
    blocks = lax.all_gather(corner, ("row", "col"), axis=0)

    owners = tile_map[:, 0] % row_count * col_count + tile_map[:, 1] % col_count
    local_ids = tile_map[:, 0] // row_count * cols_local + tile_map[:, 1] // col_count
    owner_hits = (owners[:, None] == jnp.arange(device_count)[None, :]).astype(jnp.int32)
    slot_rank = jnp.sum(jnp.cumsum(owner_hits, 0) * owner_hits, 1) - 1
    slot_index = owners * CAP + slot_rank
    packed = jnp.zeros((device_count * CAP, TILE, TILE), jnp.bfloat16).at[slot_index].set(child_tiles)
    targets = jnp.full((device_count * CAP,), -1, jnp.int32).at[slot_index].set(local_ids)
    exchange = functools.partial(
        lax.all_to_all, axis_name=("row", "col"), split_axis=0, concat_axis=0, tiled=True
    )
    arrived = exchange(packed.reshape(device_count, CAP, TILE, TILE))
    ids = exchange(targets.reshape(device_count, CAP)).reshape(device_count * CAP)
    arrived = arrived.reshape(device_count * CAP, TILE, TILE)
    tile_rows = jnp.where(ids < 0, rows_local, ids // cols_local)
    tile_cols = jnp.where(ids < 0, 0, ids % cols_local)

    panel_ids = jnp.where((ids >= 0) & (tile_cols < corner_cols), tile_rows * corner_cols + tile_cols, -1)
    selector = (panel_ids[None, :] == jnp.arange(rows_local * corner_cols)[:, None]).astype(jnp.bfloat16)
    added = jnp.dot(
        selector, arrived.reshape(device_count * CAP, TILE * TILE), preferred_element_type=jnp.float32
    )
    added = added.reshape(rows_local, corner_cols, TILE, TILE).transpose(0, 2, 1, 3)
    panel_part = (front4[:, :, :corner_cols, :].astype(jnp.float32) + added).astype(jnp.bfloat16)
    panel_part = panel_part.reshape(rows_local * TILE, width)

    row_parts = lax.all_gather(panel_part, "col", axis=0)
    all_rows = lax.all_gather(panel_part.reshape(rows_local, TILE, width), "row", axis=1)
    by_col = all_rows.reshape(cols_local, col_count, TILE, width)
    by_col = by_col[corner_cols:].transpose(1, 0, 2, 3).reshape(col_count, (cols_local - corner_cols) * TILE, width)
    col_parts = lax.all_to_all(by_col, "col", split_axis=0, concat_axis=0, tiled=True)

    lower, high, low = factor_corner(blocks, row_count, col_count)
    row_panel = solve_rows(row_parts, high, low, corner_rows * TILE)
    col_panel = solve_rows(col_parts, high, low, 0)

    top = lax.dynamic_index_in_dim(
        lower.reshape(corner_rows, row_count, TILE, PANEL), row_index, 1, keepdims=False
    ).reshape(corner_rows * TILE, PANEL)
    own = jnp.concatenate(
        [
            lax.dynamic_index_in_dim(x.reshape(-1, corner_cols, col_count, TILE), col_index, 2, keepdims=False)
            for x in (top, row_panel)
        ],
        0,
    ).reshape(rows_local * TILE, width)

    place = jnp.arange(device_count * CAP)
    before = (tile_rows[None, :] < tile_rows[:, None]) | (
        (tile_rows[None, :] == tile_rows[:, None]) & (place[None, :] < place[:, None])
    )
    rank = jnp.sum(before.astype(jnp.int32), 1)
    picked = (rank[None, :] == place[:, None]).astype(jnp.int32)
    order = jnp.sum(picked * place[None, :], 1)
    spots = jnp.sum(picked * tile_cols[None, :], 1)
    starts = jnp.sum((tile_rows[None, :] < jnp.arange(rows_local + 1)[:, None]).astype(jnp.int32), 1)
    result = trailing_update(
        row_panel,
        col_panel,
        front.reshape(rows_local * TILE, cols_local, TILE),
        own,
        arrived,
        starts,
        order,
        spots,
        corner_rows,
        corner_cols,
    )
    return result.reshape(rows_local, 1, TILE, cols_local, 1, TILE)


def solution(mesh):
    in_specs = (
        P(None, "row", None, None, "col", None),
        P(("row", "col"), None, None),
        P(("row", "col"), None),
    )
    out_specs = P(None, "row", None, None, "col", None)
    return jax.shard_map(
        per_device, mesh=mesh, in_specs=in_specs, out_specs=out_specs, check_vma=False
    )
```

time: 1570 us -> 729 us (0.46)
  other arithmetic: 616 us -> 6.29 us
  Pallas kernels: 0 us -> 319 us
  matrix products: 226 us -> 5.52 us
  waiting for transfers between devices: 476 us -> 272 us
  local copies, waits for them, and re-layouts: 199 us -> 93.3 us
    another operation x65 -> x0, other arithmetic: 530 us -> none  [the longest x62 356 us: per_device(): jnp.linalg.cholesky(corner.reshape(PANEL, PANEL).astype(jnp.float32))]
    pallas_call x0 -> x4, Pallas kernels: none -> 319 us  [the longest x1 170 us: factor_corner(): pl.pallas_call(functools.partial(factor_kernel, row_count, col_count), ou...]
    psum x1 -> x0, waiting for transfers between devices: 257 us -> none  [spread(): return lax.psum(block, axis)]
    another operation x61 -> x0, matrix products: 179 us -> none  [the longest x30 92.2 us: per_device(): jnp.linalg.cholesky(corner.reshape(PANEL, PANEL).astype(jnp.float32))]
    all_gather x3, waiting for transfers between devices: 139 us -> 243 us  [the longest x1 137 us: per_device(): lax.all_gather(panel_part.reshape(rows_local, TILE, width), 'row', axis=1)]
    another operation x80 -> x4, local copies, waits for them, and re-layouts: 79 us -> 13 us  [the longest x2 8.01 us: per_device(): row_parts = lax.all_gather(panel_part, 'col', axis=0)]
    all_to_all x3, waiting for transfers between devices: 80.3 us -> 28.6 us  [the longest x1 28.6 us: per_device(): arrived = exchange(packed.reshape(device_count, CAP, TILE, TILE))]
    dot_general x2 -> x1, matrix products: 47.7 us -> 5.52 us  [per_device(): jnp.dot(selector, arrived.reshape(device_count * CAP, TILE * TILE), prefe...]
  transfers between devices with their start and end apart: 7 -> 6, of which waited for: 6 -> 3; matrix products, arithmetic and copies ran while one was open for 4% -> 7% of each run, Pallas kernels for 0% -> 27%
where the time goes in v1:
time: 729 us; the launch traced here: 727 us
  Pallas kernels  319 us (44%)
  waiting for transfers between devices  272 us (37%)
  local copies, waits for them, and re-layouts  93.3 us (13%)
  starting transfers between devices  17.4 us (2%)
  between operations  13.3 us (2%)
    pallas_call x1, Pallas kernels, factor_corner(): pl.pallas_call(functools.partial(factor_kernel, row_count, col_count), ou...  170 us
    all_gather x1, waiting for transfers between devices, per_device(): lax.all_gather(panel_part.reshape(rows_local, TILE, width), 'row', axis=1)  137 us
    all_gather x1, waiting for transfers between devices, per_device(): blocks = lax.all_gather(corner, ('row', 'col'), axis=0)  106 us
    pallas_call x1, Pallas kernels, trailing_update(): pl.pallas_call(functools.partial(trailing_kernel, corner_rows, corner_col...  79 us
    pallas_call x2, Pallas kernels, solve_rows(): pl.pallas_call(functools.partial(solve_kernel, col_count), grid=((rows -...  70.3 us
    unnamed x11, local copies, waits for them, and re-layouts  37.9 us
    all_to_all x1, waiting for transfers between devices, per_device(): arrived = exchange(packed.reshape(device_count, CAP, TILE, TILE))  28.6 us
    dynamic_slice x3, local copies, waits for them, and re-layouts, per_device(): lax.dynamic_index_in_dim(x.reshape(-1, corner_cols, col_count, TILE), col...  16 us
  transfers between devices with their start and end apart: 6, of which 3 were waited for; matrix products, arithmetic and copies ran while one was open for 7% of the time, Pallas kernels for 27%

profile of v1, /device:TPU:2, one launch (start us, length us, event | category | flops | bytes accessed | tf_op | source)
XLA Modules:
  0.0 727.1 jit_solution(16622577092372534891)
XLA Ops:
  6.5 0.8 fusion.21
  7.3 0.8 fusion.16
  8.4 0.8 fusion.15
  9.9 0.7 all_to_all.12
  10.6 6.1 all-to-all-start
  16.7 1.9 broadcast_in_dim.13
  18.6 4.6 scatter_fusion
  23.2 5.8 all-to-all-start.1
  29.0 18.6 %copy.93 = bf16[32,1,128,16,1,128]{5,0,2,3,4,1:T(8,128)(2,1)} copy(bf16[32,1,128,16,1,128]{5,3,4,2,1,0:T(8,128)(2,1)} %param.3) | data formatting | bytes 33554432 | tf_op args[0]
  48.9 28.6 %all-to-all-done.1 = bf16[32,2,128,128]{3,2,1,0:T(8,128)(2,1)S(1)} async-done(((bf16[32,2,128,128]{3,2,1,0:T(8,128)(2,1)}), bf16[32,2,128,128]{3,2,1,0:T(8,128)(2,1)S(1)}, u32[]{:S(2)}, u32[]{:S(2)}) %all-to-all-start.1) | async-done | bytes 2097184 | tf_op jit(solution)/shard_map/all_to_all | solution.py:312
  77.5 5.5 fusion
  83.0 4.3 copy.64
  87.3 4.1 copy.65
  91.5 1.2 slice.27
  93.0 0.9 all_gather_reshape.7
  94.0 3.5 copy.74
  97.4 4.5 reshape.206
  102.8 0.7 select_reduce_fusion
  103.5 137.2 %all-gather.8.cloned.1.call-done = bf16[32,4,128,256]{3,2,0,1:T(8,128)(2,1)} async-done(((bf16[32,1,128,256]{3,2,0,1:T(8,128)(2,1)}), bf16[32,4,128,256]{3,2,0,1:T(8,128)(2,1)}) %all-gather.8.cloned.1.call-update) | async-done | bytes 8388624 | tf_op jit(solution)/shard_map/all_gather | solution.py:328
  240.7 3.1 slice-done
  243.8 4.0 copy.76
  247.8 7.2 copy.67
  255.0 5.3 all-to-all-start.2
  260.3 106.2 %all-gather.6.cloned.1.call-done.blocks_ref = bf16[32,512,256]{2,1,0:T(8,128)(2,1)} async-done(((bf16[1,512,256]{2,1,0:T(8,128)(2,1)}), bf16[32,512,256]{2,1,0:T(8,128)(2,1)}) %all-gather.6.cloned.1.call-update) | async-done | bytes 8388624 | tf_op jit(solution)/shard_map/all_gather | solution.py:300
  366.5 170.0 %factor_corner.1 = (bf16[2048,2048]{1,0:T(8,128)(2,1)}, bf16[2048,2048]{1,0:T(8,128)(2,1)}, bf16[2048,2048]{1,0:T(8,128)(2,1)}) custom-call(bf16[32,512,256]{2,1,0:T(8,128)(2,1)} %all-gather.6.cloned.1.call-done.blocks_ref), custom_call_target="tpu_custom_call" | custom-call | flops 199999995904 | bytes 33554432 | tf_op jit(solution)/shard_map/factor_corner/pallas_call | solution.py:165
  536.5 1.7 constant_dynamic-slice_fusion.1
  540.3 25.8 %solve_rows.3.xc_ref = bf16[1792,2048]{1,0:T(8,128)(2,1)} custom-call(bf16[8,1792,256]{2,1,0:T(8,128)(2,1)} %all-to-all-done.2.parts_ref, bf16[2048,2048]{1,0:T(8,128)(2,1)} %get-tuple-element.8.high_ref, bf16[2048,2048]{1,0:T(8,128)(2,1)} %get-tuple-element.9.low_ref), custom_call_target="tpu_custom_call" | custom-call | flops 15032385536 | bytes 14680064 | tf_op jit(solution)/shard_map/solve_rows/pallas_call | solution.py:201
  566.0 44.6 %solve_rows.2.xr_ref = bf16[3584,2048]{1,0:T(8,128)(2,1)} custom-call(bf16[8,4096,256]{2,1,0:T(8,128)(2,1)} %all-gather.4.cloned.1.call-done.parts_ref, bf16[2048,2048]{1,0:T(8,128)(2,1)} %get-tuple-element.8.high_ref, bf16[2048,2048]{1,0:T(8,128)(2,1)} %get-tuple-element.9.low_ref), custom_call_target="tpu_custom_call" | custom-call | flops 30064771072 | bytes 29360128 | tf_op jit(solution)/shard_map/solve_rows/pallas_call | solution.py:201
  610.6 14.5 %copy.82 = bf16[448,8,16,128]{3,2,1,0:T(8,128)(2,1)} copy(bf16[448,8,16,128]{3,1,2,0:T(8,128)(2,1)} %bitcast.86) | data formatting | bytes 29360128
  625.0 14.8 %dynamic-slice_reduce_fusion = bf16[3584,2,128]{2,1,0:T(2,128)(2,1)S(1)} fusion(bf16[3584,2,8,128]{3,2,1,0:T(8,128)(2,1)} %bitcast.89, s32[]{:T(128)S(6)} %select_n.111), kind=kLoop, calls=%fused_computation.5 | loop fusion | bytes 3670020 | tf_op jit(solution)/shard_map/jit(dynamic_index_in_dim)/dynamic_slice | solution.py:342
  640.1 1.5 pad_maximum_fusion.own_ref
  641.5 79.0 %trailing_update.1 = f32[4096,16,128]{2,1,0:T(8,128)} custom-call(s32[33]{0:T(128)} %convert_reduce_fusion.1.starts, s32[64]{0:T(128)} %get-tuple-element.12.order, s32[64]{0:T(128)} %get-tuple-element.11.spots, bf16[3584,2048]{1,0:T(8,128)(2,1)} %solve_rows.2.xr_ref, bf16[1792,2048]{1,0:T(8,128)(2,1)} %solve_rows.3.xc_ref, bf16[4096,16,128]{2,1,0:T(8,128)(2,1)} %bitcast.85, ...), custom_call_target="tpu_custom_call" | custom-call | tf_op jit(solution)/shard_map/trailing_update/pallas_call | solution.py:265
  (33 shorter events, 5.8 us)
Async XLA Ops:
  6.5 12.0 %copy-start.2 = (bf16[32,128,128]{2,1,0:T(8,128)(2,1)S(1)}, bf16[32,128,128]{2,1,0:T(8,128)(2,1)}, u32[]{:S(2)}) copy-start(bf16[32,128,128]{2,1,0:T(8,128)(2,1)} %param.4) | copy-start | bytes 3145732
  10.6 12.6 %all-to-all-start = ((s32[32,1,2]{2,1,0:T(1,128)}), s32[32,1,2]{2,1,0:T(1,128)S(1)}, u32[]{:S(2)}, u32[]{:S(2)}) async-start(s32[32,1,2]{2,1,0:T(1,128)} %bitcast.5), calls=%async_computation | async-start | bytes 32768 | tf_op jit(solution)/shard_map/all_to_all | solution.py:313
  23.2 54.3 %all-to-all-start.1 = ((bf16[32,2,128,128]{3,2,1,0:T(8,128)(2,1)}), bf16[32,2,128,128]{3,2,1,0:T(8,128)(2,1)S(1)}, u32[]{:S(2)}, u32[]{:S(2)}) async-start(bf16[32,2,128,128]{3,2,1,0:T(8,128)(2,1)} %bitcast.9), calls=%async_computation.1 | async-start | bytes 4194304 | tf_op jit(solution)/shard_map/all_to_all | solution.py:312
  29.0 211.7 %all-gather.8.cloned.1.call-start = ((), (), s32[]{:S(2)}) async-start(), calls=%async_computation.5 | async-start | bytes 10485760 | tf_op jit(solution)/shard_map/all_gather | solution.py:328
  77.5 5.5 copy-start
  91.4 2.5 copy-start.1
  91.4 275.1 %all-gather.6.cloned.1.call-start = ((), (), s32[]{:S(2)}) async-start(), calls=%async_computation.4 | async-start | bytes 8650752 | tf_op jit(solution)/shard_map/all_gather | solution.py:300
  93.9 472.1 %all-gather.4.cloned.1.call-start = ((), (), s32[]{:S(2)}) async-start(), calls=%async_computation.3 | async-start | bytes 18874368 | tf_op jit(solution)/shard_map/all_gather | solution.py:327
  240.7 3.1 slice-start
  255.0 285.3 %all-to-all-start.2 = ((bf16[8,1792,256]{2,1,0:T(8,128)(2,1)}), bf16[8,1792,256]{2,1,0:T(8,128)(2,1)}, u32[]{:S(2)}, u32[]{:S(2)}) async-start(bf16[8,1792,256]{2,1,0:T(8,128)(2,1)} %bitcast.87), calls=%async_computation.2 | async-start | bytes 14680064 | tf_op jit(solution)/shard_map/all_to_all | solution.py:331
Sparse Core Ops, SparseCore 0:
  91.6 149.1 all-gather.7
  243.6 122.9 all-gather.5
  368.4 88.3 all-gather.3

commit v2 on v1

--- a/solution.py
+++ b/solution.py
@@ -324,13 +324,16 @@
     panel_part = (front4[:, :, :corner_cols, :].astype(jnp.float32) + added).astype(jnp.bfloat16)
     panel_part = panel_part.reshape(rows_local * TILE, width)
 
+    panel_part, blocks = lax.optimization_barrier((panel_part, blocks))
+    lower, high, low = factor_corner(blocks, row_count, col_count)
+
     row_parts = lax.all_gather(panel_part, "col", axis=0)
     all_rows = lax.all_gather(panel_part.reshape(rows_local, TILE, width), "row", axis=1)
+    all_rows, lower, high, low = lax.optimization_barrier((all_rows, lower, high, low))
     by_col = all_rows.reshape(cols_local, col_count, TILE, width)
     by_col = by_col[corner_cols:].transpose(1, 0, 2, 3).reshape(col_count, (cols_local - corner_cols) * TILE, width)
     col_parts = lax.all_to_all(by_col, "col", split_axis=0, concat_axis=0, tiled=True)
 
-    lower, high, low = factor_corner(blocks, row_count, col_count)
     row_panel = solve_rows(row_parts, high, low, corner_rows * TILE)
     col_panel = solve_rows(col_parts, high, low, 0)
 

time: 729 us -> 667 us (0.915)
  waiting for transfers between devices: 272 us -> 200 us
  local copies, waits for them, and re-layouts: 93.3 us -> 104 us
    all_gather x1, waiting for transfers between devices: 137 us -> 0.01 us  [per_device(): lax.all_gather(panel_part.reshape(rows_local, TILE, width), 'row', axis=1)]
    all_to_all x1, waiting for transfers between devices: 0.01 us -> 120 us  [per_device(): lax.all_to_all(by_col, 'col', split_axis=0, concat_axis=0, tiled=True)]
    all_gather x1, waiting for transfers between devices: 106 us -> 0.02 us  [per_device(): blocks = lax.all_gather(corner, ('row', 'col'), axis=0)]
    all_to_all x1, waiting for transfers between devices: 28.6 us -> 79.9 us  [per_device(): arrived = exchange(packed.reshape(device_count, CAP, TILE, TILE))]
    all_gather x0 -> x1, local copies, waits for them, and re-layouts: none -> 22.4 us  [per_device(): row_parts = lax.all_gather(panel_part, 'col', axis=0)]
    another operation x2 -> x0, local copies, waits for them, and re-layouts: 8.01 us -> none  [per_device(): row_parts = lax.all_gather(panel_part, 'col', axis=0)]
    unnamed x11 -> x19, local copies, waits for them, and re-layouts: 37.9 us -> 38.9 us
  transfers between devices with their start and end apart: 6 -> 6, of which waited for: 3 -> 2; matrix products, arithmetic and copies ran while one was open for 7% -> 5% of each run, Pallas kernels for 27% -> 30%
where the time goes in v2:
time: 667 us; the launch traced here: 663 us
  Pallas kernels  318 us (48%)
  waiting for transfers between devices  200 us (30%)
  local copies, waits for them, and re-layouts  104 us (16%)
  starting transfers between devices  17.7 us (3%)
  between operations  13.3 us (2%)
    pallas_call x1, Pallas kernels, factor_corner(): pl.pallas_call(functools.partial(factor_kernel, row_count, col_count), ou...  170 us
    all_to_all x1, waiting for transfers between devices, per_device(): lax.all_to_all(by_col, 'col', split_axis=0, concat_axis=0, tiled=True)  120 us
    all_to_all x1, waiting for transfers between devices, per_device(): arrived = exchange(packed.reshape(device_count, CAP, TILE, TILE))  79.9 us
    pallas_call x1, Pallas kernels, trailing_update(): pl.pallas_call(functools.partial(trailing_kernel, corner_rows, corner_col...  77.8 us
    pallas_call x2, Pallas kernels, solve_rows(): pl.pallas_call(functools.partial(solve_kernel, col_count), grid=((rows -...  70.6 us
    unnamed x19, local copies, waits for them, and re-layouts  38.9 us
    all_gather x1, local copies, waits for them, and re-layouts, per_device(): row_parts = lax.all_gather(panel_part, 'col', axis=0)  22.4 us
    dynamic_slice x3, local copies, waits for them, and re-layouts, per_device(): lax.dynamic_index_in_dim(x.reshape(-1, corner_cols, col_count, TILE), col...  16 us
  transfers between devices with their start and end apart: 6, of which 2 were waited for; matrix products, arithmetic and copies ran while one was open for 5% of the time, Pallas kernels for 30%

profile of v2, /device:TPU:2, one launch (start us, length us, event | category | flops | bytes accessed | tf_op | source)
XLA Modules:
  0.0 663.3 jit_solution(5302447706090248385)
XLA Ops:
  6.5 14.8 %copy.88 = bf16[32,1,128,16,1,128]{5,0,2,3,4,1:T(8,128)(2,1)S(1)} copy(bf16[32,1,128,16,1,128]{5,3,4,2,1,0:T(8,128)(2,1)} %param.3) | data formatting | bytes 33554432 | tf_op args[0]
  21.4 6.1 copy-done.1
  27.9 0.9 all_gather_reshape.6
  29.2 0.7 scatter_custom_fusion
  29.8 0.7 all_to_all.12
  30.5 6.1 all-to-all-start
  36.7 1.9 broadcast_in_dim.13
  38.5 4.6 scatter_fusion
  43.2 5.8 all-to-all-start.1
  49.6 0.6 reduce.5
  50.8 79.9 %all-to-all-done.1 = bf16[32,2,128,128]{3,2,1,0:T(8,128)(2,1)S(1)} async-done(((bf16[32,2,128,128]{3,2,1,0:T(8,128)(2,1)}), bf16[32,2,128,128]{3,2,1,0:T(8,128)(2,1)S(1)}, u32[]{:S(2)}, u32[]{:S(2)}) %all-to-all-start.1) | async-done | bytes 2097184 | tf_op jit(solution)/shard_map/all_to_all | solution.py:312
  130.7 5.7 fusion
  136.4 5.1 copy.58
  141.5 2.6 copy.89
  144.1 2.7 copy.69
  147.5 169.8 %factor_corner.1 = (bf16[2048,2048]{1,0:T(8,128)(2,1)}, bf16[2048,2048]{1,0:T(8,128)(2,1)}, bf16[2048,2048]{1,0:T(8,128)(2,1)}) custom-call(bf16[32,512,256]{2,1,0:T(8,128)(2,1)} %all-gather.5.cloned.1.call-done.blocks_ref), custom_call_target="tpu_custom_call" | custom-call | flops 199999995904 | bytes 33554432 | tf_op jit(solution)/shard_map/factor_corner/pallas_call | solution.py:165
  317.3 3.1 slice-done
  320.4 3.9 copy.62
  324.3 5.5 all-to-all-start.2
  329.8 0.6 convert_reduce_fusion.1.starts
  330.6 0.7 select_reduce_fusion
  331.4 1.7 constant_dynamic-slice_fusion.1
  333.1 0.6 copy.75
  334.3 0.7 copy.64
  335.1 120.0 %all-to-all-done.2.parts_ref = bf16[8,1792,256]{2,1,0:T(8,128)(2,1)} async-done(((bf16[8,1792,256]{2,1,0:T(8,128)(2,1)}), bf16[8,1792,256]{2,1,0:T(8,128)(2,1)}, u32[]{:S(2)}, u32[]{:S(2)}) %all-to-all-start.2) | async-done | bytes 7340064 | tf_op jit(solution)/shard_map/all_to_all | solution.py:335
  455.1 26.0 %solve_rows.3.xc_ref = bf16[1792,2048]{1,0:T(8,128)(2,1)} custom-call(bf16[8,1792,256]{2,1,0:T(8,128)(2,1)} %all-to-all-done.2.parts_ref, bf16[2048,2048]{1,0:T(8,128)(2,1)} %get-tuple-element.19.high_ref, bf16[2048,2048]{1,0:T(8,128)(2,1)} %get-tuple-element.20.low_ref), custom_call_target="tpu_custom_call" | custom-call | flops 15032385536 | bytes 14680064 | tf_op jit(solution)/shard_map/solve_rows/pallas_call | solution.py:201
  481.2 22.4 %copy.60 = bf16[32768,256]{1,0:T(8,128)(2,1)} copy(bf16[32768,256]{0,1:T(8,128)(2,1)} %all-gather.9.cloned.1.call-done) | data formatting | bytes 33554432 | tf_op jit(solution)/shard_map/all_gather | solution.py:330
  503.5 44.5 %solve_rows.2.xr_ref = bf16[3584,2048]{1,0:T(8,128)(2,1)} custom-call(bf16[8,4096,256]{2,1,0:T(8,128)(2,1)} %bitcast.102, bf16[2048,2048]{1,0:T(8,128)(2,1)} %get-tuple-element.19.high_ref, bf16[2048,2048]{1,0:T(8,128)(2,1)} %get-tuple-element.20.low_ref), custom_call_target="tpu_custom_call" | custom-call | flops 30064771072 | bytes 29360128 | tf_op jit(solution)/shard_map/solve_rows/pallas_call | solution.py:201
  548.0 14.5 %copy.76 = bf16[448,8,16,128]{3,2,1,0:T(8,128)(2,1)} copy(bf16[448,8,16,128]{3,1,2,0:T(8,128)(2,1)} %bitcast.94) | data formatting | bytes 29360128
  562.5 14.8 %dynamic-slice_reduce_fusion = bf16[3584,2,128]{2,1,0:T(2,128)(2,1)S(1)} fusion(bf16[3584,2,8,128]{3,2,1,0:T(8,128)(2,1)} %bitcast.97, s32[]{:T(128)S(6)} %select_n.111), kind=kLoop, calls=%fused_computation.5 | loop fusion | bytes 3670020 | tf_op jit(solution)/shard_map/jit(dynamic_index_in_dim)/dynamic_slice | solution.py:345
  577.5 1.5 pad_maximum_fusion.own_ref
  579.0 77.8 %trailing_update.1 = f32[4096,16,128]{2,1,0:T(8,128)} custom-call(s32[33]{0:T(128)} %convert_reduce_fusion.1.starts, s32[64]{0:T(128)} %get-tuple-element.24.order, s32[64]{0:T(128)} %get-tuple-element.23.spots, bf16[3584,2048]{1,0:T(8,128)(2,1)} %solve_rows.2.xr_ref, bf16[1792,2048]{1,0:T(8,128)(2,1)} %solve_rows.3.xc_ref, bf16[4096,16,128]{2,1,0:T(8,128)(2,1)} %bitcast.93, ...), custom_call_target="tpu_custom_call" | custom-call | tf_op jit(solution)/shard_map/trailing_update/pallas_call | solution.py:265
  (40 shorter events, 3.8 us)
Async XLA Ops:
  6.5 22.2 %copy-start.5 = (s32[32,2]{0,1:T(2,128)S(1)}, s32[32,2]{0,1:T(2,128)}, u32[]{:S(2)}) copy-start(s32[32,2]{0,1:T(2,128)} %param.5) | copy-start | bytes 772
  6.5 137.5 %all-gather.5.cloned.1.call-start = ((), (), s32[]{:S(2)}) async-start(), calls=%async_computation.3 | async-start | bytes 8650752 | tf_op jit(solution)/shard_map/all_gather | solution.py:300
  21.3 6.2 copy-start.1
  21.4 17.2 %copy-start.3 = (bf16[32,128,128]{2,1,0:T(8,128)(2,1)S(1)}, bf16[32,128,128]{2,1,0:T(8,128)(2,1)}, u32[]{:S(2)}) copy-start(bf16[32,128,128]{2,1,0:T(8,128)(2,1)} %param.4) | copy-start | bytes 3145732
  30.5 12.6 %all-to-all-start = ((s32[32,1,2]{2,1,0:T(1,128)}), s32[32,1,2]{2,1,0:T(1,128)S(1)}, u32[]{:S(2)}, u32[]{:S(2)}) async-start(s32[32,1,2]{2,1,0:T(1,128)} %bitcast.5), calls=%async_computation | async-start | bytes 32768 | tf_op jit(solution)/shard_map/all_to_all | solution.py:313
  43.2 87.5 %all-to-all-start.1 = ((bf16[32,2,128,128]{3,2,1,0:T(8,128)(2,1)}), bf16[32,2,128,128]{3,2,1,0:T(8,128)(2,1)S(1)}, u32[]{:S(2)}, u32[]{:S(2)}) async-start(bf16[32,2,128,128]{3,2,1,0:T(8,128)(2,1)} %bitcast.9), calls=%async_computation.1 | async-start | bytes 4194304 | tf_op jit(solution)/shard_map/all_to_all | solution.py:312
  49.0 268.3 %all-gather.7.cloned.1.call-start = ((), (), s32[]{:S(2)}) async-start(), calls=%async_computation.4 | async-start | bytes 10485760 | tf_op jit(solution)/shard_map/all_gather | solution.py:331
  130.7 5.7 copy-start.2
  144.0 2.7 copy-start
  146.8 334.4 %all-gather.9.cloned.1.call-start = ((), (), s32[]{:S(2)}) async-start(), calls=%async_computation.5 | async-start | bytes 18874368 | tf_op jit(solution)/shard_map/all_gather | solution.py:330
  317.3 3.1 slice-start
  324.3 5.5 copy-start.6
  324.3 6.3 copy-start.4
  324.3 130.8 %all-to-all-start.2 = ((bf16[8,1792,256]{2,1,0:T(8,128)(2,1)}), bf16[8,1792,256]{2,1,0:T(8,128)(2,1)}, u32[]{:S(2)}, u32[]{:S(2)}) async-start(bf16[8,1792,256]{2,1,0:T(8,128)(2,1)} %bitcast.95), calls=%async_computation.2 | async-start | bytes 14680064 | tf_op jit(solution)/shard_map/all_to_all | solution.py:335
Sparse Core Ops, SparseCore 0:
  28.9 104.5 all-gather.4
  146.9 149.5 all-gather.6
  298.4 160.1 all-gather.8
